TPU v7x, 32 devices: a whole 2x2x4 slice. The times are simulated.
32 devices in a mesh: los: 2 (over x), tx: 4 (over y, core), ty: 4 (over z).
Axes of the slice: x: 2, y: 2, z: 4, core: 2. Of those that a mesh axis runs over, the one named last changes fastest.
Arguments:
- kappa_cot: float32 [4, 2048, 2048], P(None, 'ty', 'tx'), may hold values from -6 to 6
- efficiency: float32 [4, 8], P(None, 'los'), may hold values from 0.1 to 1
- interp_x: bfloat16 [8, 2048, 1024], P('los', 'ty'), may hold values from -0.125 to 0.125
- interp_y: bfloat16 [8, 2048, 1024], P('los', 'tx'), may hold values from -0.125 to 0.125
- plane_shell: int32 [512], replicated, may hold values from 0 to 7, as said below
Outputs:
- density_cot: bfloat16 [2, 512, 1024, 1024], P(None, 'los', 'ty', 'tx')
Inputs may be any that keep to these rules, and one draw needn't show every extreme that they name: `plane_shell`: non-decreasing along the 512 planes; each of the 8 shells holds one or more consecutive planes.
All inputs are finite; a program needn't handle non-finite values.
Results may differ from a plain program's by a relative error of at most 0.0049.
Values sent between devices are 32-bit elements; how exact they have to be, the bound alone decides.
A program may use at most 256 MiB of HBM per device.

v0:
```python
import math

import jax
import jax.numpy as jnp
from jax import lax
from jax.sharding import PartitionSpec as P

NSHELL = 8
NX = 1024
NY = 1024
NZ = 512


highest = lax.Precision.HIGHEST


def phasor_table(first_row, row_count, length):
    wave_rows = first_row + jnp.arange(row_count, dtype=jnp.int32)
    positions = jnp.arange(length, dtype=jnp.int32)
    phase = wave_rows[:, None] * positions[None, :] % length
    angle = phase.astype(jnp.float32) * (2.0 * math.pi / length)
    factor = 1.0 / math.sqrt(length)
    return (jnp.cos(angle) * factor, -jnp.sin(angle) * factor)


def transform_real(source, first_row, row_count, length):
    cosine, sine_neg = phasor_table(first_row, row_count, length)
    cosine_part = jnp.dot(cosine, source, precision=highest, preferred_element_type=jnp.float32)
    sine_part = jnp.dot(sine_neg, source, precision=highest, preferred_element_type=jnp.float32)
    return (cosine_part, sine_part)


def transform_pairs(source, first_row, row_count, length):
    cosine_part, sine_part = transform_real(
        source.reshape(length, -1), first_row, row_count, length
    )
    cosine_part = cosine_part.reshape(row_count, -1, 2)
    sine_part = sine_part.reshape(row_count, -1, 2)
    real_part = cosine_part[..., 0] - sine_part[..., 1]
    imag_part = cosine_part[..., 1] + sine_part[..., 0]
    return (real_part, imag_part)


def body(kappa_cot, efficiency, interp_x, interp_y, plane_shell):
    weighted = jnp.einsum("bs,buv->suv", efficiency, kappa_cot, precision=highest).astype(
        jnp.bfloat16
    )
    shells_here = weighted.shape[0]
    pix_cols = weighted.shape[2]
    kx_rows = NX // lax.axis_size("ty")
    ky_rows = NY // lax.axis_size("tx")
    projected = jnp.einsum(
        "sui,suv->isv", interp_x, weighted, preferred_element_type=jnp.float32
    ).reshape(NX, shells_here * pix_cols)
    cosine_part, sine_part = transform_real(
        projected, jnp.int32(0), kx_rows * lax.axis_size("ty"), NX
    )
    row_spectra = lax.psum_scatter(
        jnp.stack(
            [
                cosine_part.reshape(kx_rows * lax.axis_size("ty"), shells_here, pix_cols),
                sine_part.reshape(kx_rows * lax.axis_size("ty"), shells_here, pix_cols),
            ],
            axis=2,
        ),
        "ty",
        scatter_dimension=0,
        tiled=True,
    )
    along_y = jnp.einsum(
        "xscv,svj->jxsc", row_spectra, interp_y.astype(jnp.float32), precision=highest
    )
    real_part, imag_part = transform_pairs(along_y, jnp.int32(0), ky_rows * lax.axis_size("tx"), NY)
    summed = lax.psum_scatter(
        jnp.stack([real_part, imag_part], axis=-1).reshape(ky_rows * lax.axis_size("tx"), -1),
        "tx",
        scatter_dimension=0,
        tiled=True,
    )
    spectra = summed.reshape(ky_rows, kx_rows, shells_here, 2).transpose(1, 2, 3, 0)
    every_shell = lax.all_gather(spectra, "los", axis=1, tiled=True)
    z_rows = NZ // lax.axis_size("los")
    cosine, sine_neg = phasor_table(lax.axis_index("los") * z_rows, z_rows, NZ)
    indicator = (plane_shell[:, None] == jnp.arange(NSHELL, dtype=jnp.int32)[None, :]).astype(
        jnp.float32
    )
    shell_real = jnp.dot(cosine, indicator, precision=highest, preferred_element_type=jnp.float32)
    shell_imag = jnp.dot(sine_neg, indicator, precision=highest, preferred_element_type=jnp.float32)
    mixing = jnp.stack(
        [
            jnp.stack([shell_real, -shell_imag], axis=-1),
            jnp.stack([shell_imag, shell_real], axis=-1),
        ]
    )
    mixed = jnp.einsum("cksd,xsdy->ckxy", mixing, every_shell, precision=highest)
    return mixed.astype(jnp.bfloat16)


def solution(mesh):
    return jax.shard_map(
        body,
        mesh=mesh,
        in_specs=(
            P(None, "ty", "tx"),
            P(None, "los"),
            P("los", "ty", None),
            P("los", "tx", None),
            P(),
        ),
        out_specs=P(None, "los", "ty", "tx"),
        check_vma=False,
    )
```

profile of v0, /device:TPU:0, one launch (start us, length us, event | category | flops | bytes accessed | tf_op | source)
XLA Modules:
  0.0 850.2 jit_solution(2956920094416960748)
XLA Ops:
  6.5 0.0 copy-start
  6.5 0.0 reduce-scatter.3.cloned.1.call-start
  6.5 0.7 copy-done
  7.2 0.0 copy-start.3
  7.2 13.8 %fusion.44 = bf16[4,512,512]{2,0,1:T(4,128)(2,1)S(1)} fusion(f32[4,512,512]{2,1,0:T(8,128)} %param.5, f32[4,4]{1,0:T(4,128)S(1)} %copy-done), kind=kOutput, calls=%fused_computation.42 | convolution fusion | flops 51380224 | bytes 6291520 | tf_op jit(solution)/shard_map/bs,buv->suv/dot_general | solution.py:45
  21.0 0.0 copy-done.3
  21.0 2.5 fusion.34
  23.5 44.1 %fusion.28 = f32[1024,4,1,512]{3,0,1,2:T(8,128)S(1)} fusion(f32[4,512,1024]{2,1,0:T(8,128)S(1)} %fusion.34), kind=kOutput, calls=%fused_computation.34 | convolution fusion | flops 25785532416 | bytes 16777216 | tf_op jit(solution)/shard_map/dot_general | solution.py:28
  67.6 54.2 %fusion.31 = f32[1024,4,1,512]{3,0,1,2:T(8,128)S(1)} fusion(f32[4,512,1024]{2,1,0:T(8,128)S(1)} %fusion.34), kind=kOutput, calls=%fused_computation.35 | convolution fusion | flops 25786580992 | bytes 16777216 | tf_op jit(solution)/shard_map/dot_general | solution.py:29
  121.9 6.4 pad_maximum_fusion
  128.2 0.0 reduce-scatter.3.cloned.1.call-update
  128.3 0.0 reduce-scatter.5.cloned.1.call-start
  128.3 16.4 %fusion.112 = f32[1024,1024,1]{1,0,2:T(8,128)} fusion(), kind=kLoop, calls=%fused_computation.21.clone.1 | loop fusion | flops 15728640 | bytes 4194304 | tf_op jit(solution)/shard_map/dot_general | solution.py:28
  144.7 16.5 %fusion.110 = f32[1024,1024,1]{1,0,2:T(8,128)} fusion(), kind=kLoop, calls=%fused_computation.18.clone.1 | loop fusion | flops 16777216 | bytes 4194304 | tf_op jit(solution)/shard_map/dot_general | solution.py:29
  161.2 250.3 %reduce-scatter.3.cloned.1.call-done = f32[256,4,2,512]{3,0,1,2:T(8,128)} async-done(((f32[1024,4,2,512]{3,0,1,2:T(8,128)}), f32[256,4,2,512]{3,0,1,2:T(8,128)}) %reduce-scatter.3.cloned.1.call-update) | async-done | bytes 4194320 | tf_op jit(solution)/shard_map/reduce_scatter | solution.py:58
  411.4 9.2 %fusion.23 = f32[1024,256,4,2]{0,1,3,2:T(8,128)S(1)} fusion(bf16[4,512,1024]{2,1,0:T(8,128)(2,1)} %param.8, f32[256,4,2,512]{3,0,1,2:T(8,128)} %reduce-scatter.3.cloned.1.call-done), kind=kOutput, calls=%fused_computation.33 | convolution fusion | flops 12884901888 | bytes 16777216 | tf_op jit(solution)/shard_map/xscv,svj->jxsc/dot_general | solution.py:70
  420.6 10.0 %copy.19 = f32[1024,256,4,2]{0,3,2,1:T(2,128)} copy(f32[1024,256,4,2]{0,1,3,2:T(8,128)S(1)} %fusion.23) | data formatting | bytes 16777216 | tf_op jit(solution)/shard_map/xscv,svj->jxsc/transpose | solution.py:70
  430.6 10.9 %reshape.33 = f32[1024,2048]{0,1:T(8,128)} reshape(f32[1024,256,4,2]{0,3,2,1:T(2,128)} %copy.19) | data formatting | bytes 16777216 | tf_op jit(solution)/shard_map/reshape | solution.py:35
  441.5 10.5 %dot_general.51 = f32[1024,2,1024]{2,1,0:T(2,128)} reshape(f32[2048,1024]{1,0:T(8,128)} %bitcast.82) | data formatting | bytes 16777216 | tf_op jit(solution)/shard_map/dot_general | solution.py:28
  452.1 0.0 copy-start.2
  452.1 0.0 copy-start.4
  452.1 34.1 %fusion = f32[1024,1024,2]{0,1,2:T(8,128)} fusion(f32[1024,2,1024]{2,1,0:T(2,128)} %dot_general.51, f32[1024,1024,1]{1,0,2:T(8,128)} %fusion.110), kind=kOutput, calls=%fused_computation.3 | convolution fusion | flops 25769803776 | bytes 20971520 | tf_op jit(solution)/shard_map/dot_general | solution.py:29
  486.2 0.0 copy-done.2
  486.2 0.0 copy-done.4
  486.2 30.0 %fusion.2 = f32[1024,1024,2]{0,1,2:T(8,128)} fusion(f32[1024,2,1024]{2,1,0:T(2,128)S(1)} %copy-done.2, f32[1024,1024,1]{1,0,2:T(8,128)S(1)} %copy-done.4), kind=kOutput, calls=%fused_computation.5 | convolution fusion | flops 25769803776 | bytes 20971520 | tf_op jit(solution)/shard_map/dot_general | solution.py:28
  516.2 10.3 %slice_subtract_fusion = (f32[1024,1024,1]{0,1,2:T(8,128)S(1)}, f32[1024,1024,1]{0,1,2:T(8,128)}) fusion(f32[1024,1024,2]{0,1,2:T(8,128)} %fusion, f32[1024,1024,2]{0,1,2:T(8,128)} %fusion.2), kind=kLoop, calls=%fused_computation.14 | loop fusion | flops 2097152 | bytes 25165824 | tf_op jit(solution)/shard_map/sub | solution.py:39
  526.5 3.2 pad_maximum_fusion.1
  529.7 13.2 %copy.22 = f32[1024,1024,2]{0,2,1:T(2,128)} copy(f32[1024,1024,2]{0,1,2:T(8,128)S(1)} %pad_maximum_fusion.1) | data formatting | bytes 16777216 | tf_op jit(solution)/shard_map/stack | solution.py:75
  542.9 10.9 %reshape.34 = f32[1024,2048]{0,1:T(8,128)} reshape(f32[1024,1024,2]{0,2,1:T(2,128)} %copy.22) | data formatting | bytes 16777216 | tf_op jit(solution)/shard_map/reshape | solution.py:75
  553.8 0.0 reduce-scatter.5.cloned.1.call-update
  553.8 0.0 all-gather.2.cloned.1.call-start
  553.9 72.5 %reduce-scatter.5.cloned.1.call-done = f32[256,2048]{0,1:T(8,128)} async-done(((f32[1024,2048]{0,1:T(8,128)}), f32[256,2048]{0,1:T(8,128)}) %reduce-scatter.5.cloned.1.call-update) | async-done | bytes 2097168 | tf_op jit(solution)/shard_map/reduce_scatter | solution.py:74
  626.4 2.5 reshape.35
  628.9 0.0 copy-start.5
  628.9 2.0 copy.23
  630.9 0.0 all-gather.2.cloned.1.call-update
  630.9 0.0 copy-done.5
  630.9 2.3 convolution_bitcast_fusion
  633.2 2.4 fusion.50
  635.7 52.1 %all-gather.2.cloned.1.call-done = f32[256,8,2,256]{3,0,2,1:T(8,128)} async-done(((f32[256,4,2,256]{3,0,2,1:T(8,128)}), f32[256,8,2,256]{3,0,2,1:T(8,128)}) %all-gather.2.cloned.1.call-update) | async-done | bytes 4194320 | tf_op jit(solution)/shard_map/all_gather | solution.py:81
  687.8 111.0 %bitcast_convert_fusion = bf16[2,256,256,256]{3,1,2,0:T(8,128)(2,1)} fusion(f32[256,8,2,256]{3,0,2,1:T(8,128)} %all-gather.2.cloned.1.call-done, f32[2,256,8,2,1]{1,2,3,4,0:T(8,128)S(1)} %maximum_bitcast_fusion.6), kind=kOutput, calls=%fused_computation | convolution fusion | flops 6476005376 | bytes 71335936 | tf_op jit(solution)/shard_map/cksd,xsdy->ckxy/dot_general | solution.py:95
  798.8 0.0 copy-start.1
  798.8 44.4 %copy.25 = bf16[2,256,256,256]{3,2,1,0:T(8,128)(2,1)} copy(bf16[2,256,256,256]{3,1,2,0:T(8,128)(2,1)} %bitcast_convert_fusion) | data formatting | bytes 134217728 | tf_op jit(solution)/shard_map/convert_element_type | solution.py:96
  843.2 0.0 copy-done.1
  (4 shorter events, 0.1 us)
Async XLA Ops:
  6.5 0.7 copy-start
  6.5 404.9 %reduce-scatter.3.cloned.1.call-start = ((), (), s32[]{:S(2)}) async-start(), calls=%async_computation.2 | async-start | bytes 20971520 | tf_op jit(solution)/shard_map/reduce_scatter | solution.py:58
  7.2 13.8 %copy-start.3 = (bf16[4,512,1024]{2,1,0:T(8,128)(2,1)S(1)}, bf16[4,512,1024]{2,1,0:T(8,128)(2,1)}, u32[]{:S(2)}) copy-start(bf16[4,512,1024]{2,1,0:T(8,128)(2,1)} %param.7) | copy-start | bytes 12582916
  128.3 498.1 %reduce-scatter.5.cloned.1.call-start = ((), (), s32[]{:S(2)}) async-start(), calls=%async_computation.3 | async-start | bytes 10485760 | tf_op jit(solution)/shard_map/reduce_scatter | solution.py:74
  452.1 34.1 %copy-start.2 = (f32[1024,2,1024]{2,1,0:T(2,128)S(1)}, f32[1024,2,1024]{2,1,0:T(2,128)}, u32[]{:S(2)}) copy-start(f32[1024,2,1024]{2,1,0:T(2,128)} %dot_general.51) | copy-start | bytes 25165828
  452.1 34.1 %copy-start.4 = (f32[1024,1024,1]{1,0,2:T(8,128)S(1)}, f32[1024,1024,1]{1,0,2:T(8,128)}, u32[]{:S(2)}) copy-start(f32[1024,1024,1]{1,0,2:T(8,128)} %fusion.112) | copy-start | bytes 12582916
  553.8 134.0 %all-gather.2.cloned.1.call-start = ((), (), s32[]{:S(2)}) async-start(), calls=%async_computation.4 | async-start | bytes 6291456 | tf_op jit(solution)/shard_map/all_gather | solution.py:81
  628.9 2.0 copy-start.5
  798.8 44.4 %copy-start.1 = (f32[4,4]{1,0:T(4,128)S(1)}, f32[4,4]{1,0:T(4,128)}, u32[]{:S(2)}) copy-start(f32[4,4]{1,0:T(4,128)} %param.6) | copy-start | bytes 196
Sparse Core Ops, SparseCore 0:
  128.4 283.0 reduce-scatter.2
  553.9 72.3 reduce-scatter.4
  631.0 56.7 all-gather.1
where the time goes:
time: 857 us; the launch traced here: 850 us
  waiting for transfers between devices  375 us (44%)
  matrix products  304 us (35%)
  local copies, waits for them, and re-layouts  105 us (12%)
  other arithmetic  52.8 us (6%)
  between operations  13.7 us (2%)
    reduce_scatter x1, waiting for transfers between devices, body(): lax.psum_scatter(jnp.stack([cosine_part.reshape(kx_rows * lax.axis_size('...  250 us
    dot_general x1, matrix products, body(): jnp.einsum('cksd,xsdy->ckxy', mixing, every_shell, precision=highest)  111 us
    dot_general x2, matrix products, transform_real(): jnp.dot(sine_neg, source, precision=highest, preferred_element_type=jnp.f...  88.3 us
    dot_general x2, matrix products, transform_real(): jnp.dot(cosine, source, precision=highest, preferred_element_type=jnp.flo...  74.2 us
    reduce_scatter x1, waiting for transfers between devices, body(): lax.psum_scatter(jnp.stack([real_part, imag_part], axis=-1).reshape(ky_ro...  72.5 us
    all_gather x1, waiting for transfers between devices, body(): every_shell = lax.all_gather(spectra, 'los', axis=1, tiled=True)  52.1 us
    convert_element_type x1, local copies, waits for them, and re-layouts, body(): return mixed.astype(jnp.bfloat16)  44.4 us
  transfers between devices with their start and end apart: 3, of which 3 were waited for; matrix products, arithmetic and copies ran while one was open for 4% of the time, Pallas kernels for 0%

commit v1 on v0

v1 whole, which is shorter than its diff:
```python
import math

import jax
import jax.numpy as jnp
import numpy as np
from jax import lax
from jax.experimental import pallas as pl
from jax.experimental.pallas import tpu as pltpu
from jax.sharding import PartitionSpec as P

NSHELL = 8
NX = 1024
NY = 1024
NZ = 512
TILE = 16

highest = lax.Precision.HIGHEST
high = lax.Precision.HIGH


def phasor_table(first_row, row_count, length):
    wave_rows = first_row + jnp.arange(row_count, dtype=jnp.int32)
    positions = jnp.arange(length, dtype=jnp.int32)
    phase = wave_rows[:, None] * positions[None, :] % length
    angle = phase.astype(jnp.float32) * (2.0 * math.pi / length)
    factor = 1.0 / math.sqrt(length)
    return (jnp.cos(angle) * factor, -jnp.sin(angle) * factor)


def wave_tables(length, groups):
    waves = np.arange(length)
    angle = (waves[:, None] * waves[None, :] % length) * (2.0 * np.pi / length)
    shape = (groups, 1, length // groups, length)
    cosine = (np.cos(angle) / np.sqrt(length)).reshape(shape)
    sine_neg = (-np.sin(angle) / np.sqrt(length)).reshape(shape)
    return cosine, sine_neg


def real_rows(length, groups):
    cosine, sine_neg = wave_tables(length, groups)
    rows = np.concatenate([cosine, sine_neg], axis=1)
    return rows.reshape(2 * length, length).astype(np.float32)


def complex_rows(length, groups):
    cosine, sine_neg = wave_tables(length, groups)
    real = np.concatenate([cosine, -sine_neg], axis=3)
    imag = np.concatenate([sine_neg, cosine], axis=3)
    rows = np.concatenate([real, imag], axis=1)
    return rows.reshape(2 * length, 2 * length).astype(np.float32)


def mix_kernel(mix_ref, spec_ref, out_ref):
    spec = spec_ref[...].astype(jnp.bfloat16)
    spec = spec.reshape(spec.shape[0] * spec.shape[1], spec.shape[2])
    chunk = out_ref.shape[0] // 8
    for part in range(8):
        mixed = jnp.dot(
            mix_ref[part * chunk * TILE : (part + 1) * chunk * TILE, :],
            spec,
            preferred_element_type=jnp.float32,
        )
        out_ref[part * chunk : (part + 1) * chunk] = mixed.astype(jnp.bfloat16).reshape(
            chunk, TILE, spec.shape[1]
        )


def spread_mixing(mixing):
    rows, terms = mixing.shape
    wide = jnp.repeat(mixing, TILE, axis=1)
    same_row = jnp.tile(jnp.eye(TILE, dtype=jnp.float32), (1, terms))
    spread = wide[:, None, :] * same_row[None, :, :]
    return spread.astype(jnp.bfloat16).reshape(rows * TILE, terms * TILE)


def mix(spread, spectra):
    rows = spread.shape[0] // TILE
    terms, kx_rows, ky_rows = spectra.shape
    return pl.pallas_call(
        mix_kernel,
        grid=(kx_rows // TILE,),
        in_specs=[
            pl.BlockSpec((rows * TILE, terms * TILE), lambda x: (0, 0)),
            pl.BlockSpec((terms, TILE, ky_rows), lambda x: (0, x, 0)),
        ],
        out_specs=pl.BlockSpec((rows, TILE, ky_rows), lambda x: (0, x, 0)),
        out_shape=jax.ShapeDtypeStruct((rows, kx_rows, ky_rows), jnp.bfloat16),
        compiler_params=pltpu.CompilerParams(vmem_limit_bytes=40 * 1024 * 1024),
    )(spread, spectra)


def halving_scatter(partial, axis):
    size = lax.axis_size(axis)
    me = lax.axis_index(axis)
    blocks = partial.reshape(size, partial.shape[0] // size, partial.shape[1])
    step = 1
    while step < size:
        bit = me // step % 2
        pairs = blocks.reshape(blocks.shape[0] // 2, 2, *blocks.shape[1:])
        keep = lax.dynamic_index_in_dim(pairs, bit, 1, keepdims=False)
        give = lax.dynamic_index_in_dim(pairs, 1 - bit, 1, keepdims=False)
        blocks = keep + lax.ppermute(give, axis, [(i, i ^ step) for i in range(size)])
        step *= 2
    return blocks[0]


def body(kappa_cot, efficiency, interp_x, interp_y, plane_shell):
    shells_here = efficiency.shape[1]
    kx_rows = NX // lax.axis_size("ty")
    ky_rows = NY // lax.axis_size("tx")
    rows_y = jnp.asarray(real_rows(NY, lax.axis_size("tx")))
    rows_x = jnp.asarray(complex_rows(NX, lax.axis_size("ty")))

    z_rows = NZ // lax.axis_size("los")
    cosine, sine_neg = phasor_table(lax.axis_index("los") * z_rows, z_rows, NZ)
    groups = lax.axis_size("los")
    sources = (lax.axis_index("los") + jnp.arange(groups, dtype=jnp.int32)) % groups
    shell_order = (
        sources[:, None] * shells_here + jnp.arange(shells_here, dtype=jnp.int32)[None, :]
    ).reshape(1, NSHELL)
    indicator = (plane_shell[:, None] == shell_order).astype(jnp.float32)
    shell_real = jnp.dot(cosine, indicator, precision=highest, preferred_element_type=jnp.float32)
    shell_imag = jnp.dot(sine_neg, indicator, precision=highest, preferred_element_type=jnp.float32)
    mixing = jnp.concatenate(
        [
            jnp.stack([shell_real, -shell_imag], axis=-1),
            jnp.stack([shell_imag, shell_real], axis=-1),
        ]
    )

    along_y = []
    for s in range(shells_here):
        weighted = sum(
            efficiency[b, s] * kappa_cot[b] for b in range(efficiency.shape[0])
        ).astype(jnp.bfloat16)
        gridded = jnp.einsum(
            "vj,uv->ju", interp_y[s], weighted, preferred_element_type=jnp.float32
        )
        partial = jnp.dot(rows_y, gridded, precision=high, preferred_element_type=jnp.float32)
        along_y.append(halving_scatter(partial, "tx"))
    spread = spread_mixing(mixing.reshape(2 * z_rows, 2 * NSHELL))
    every_shell = [[] for _ in range(groups)]
    for s in range(shells_here):
        columns = along_y[s].reshape(2, ky_rows, -1)
        gridded = jnp.einsum(
            "ui,cyu->ciy",
            interp_x[s].astype(jnp.float32),
            columns,
            precision=high,
            preferred_element_type=jnp.float32,
        ).reshape(2 * NX, ky_rows)
        partial = jnp.dot(rows_x, gridded, precision=high, preferred_element_type=jnp.float32)
        summed = lax.psum_scatter(partial, "ty", scatter_dimension=0, tiled=True)
        summed = summed.reshape(2, kx_rows, ky_rows)
        every_shell[0].append(summed)
        for shift in range(1, groups):
            moves = [((i + shift) % groups, i) for i in range(groups)]
            every_shell[shift].append(lax.ppermute(summed, "los", moves))
    spectra = jnp.concatenate([block for group in every_shell for block in group])
    mixed = mix(spread, spectra)
    return mixed.reshape(2, z_rows, kx_rows, ky_rows)


def solution(mesh):
    return jax.shard_map(
        body,
        mesh=mesh,
        in_specs=(
            P(None, "ty", "tx"),
            P(None, "los"),
            P("los", "ty", None),
            P("los", "tx", None),
            P(),
        ),
        out_specs=P(None, "los", "ty", "tx"),
        check_vma=False,
    )
```

time: 857 us -> 325 us (0.38)
  waiting for transfers between devices: 375 us -> 85.3 us
  matrix products: 304 us -> 134 us
  local copies, waits for them, and re-layouts: 105 us -> 31.4 us
  other arithmetic: 52.8 us -> 16.5 us
  Pallas kernels: 0 us -> 27.7 us
  starting transfers between devices: 0.09 us -> 12.4 us
    reduce_scatter x2 -> x4, waiting for transfers between devices: 323 us -> 39.5 us  [body(): summed = lax.psum_scatter(partial, 'ty', scatter_dimension=0, tiled=True)]
    dot_general x8 -> x16, matrix products: 299 us -> 129 us  [the longest x4 57.9 us: body(): jnp.dot(rows_x, gridded, precision=high, preferred_element_type=jnp.float32)]
    all_gather x1 -> x0, waiting for transfers between devices: 52.1 us -> none  [body(): every_shell = lax.all_gather(spectra, 'los', axis=1, tiled=True)]
    ppermute x0 -> x12, waiting for transfers between devices: none -> 45.7 us  [the longest x8 41.6 us: halving_scatter(): lax.ppermute(give, axis, [(i, i ^ step) for i in range(size)])]
    convert_element_type x1 -> x0, local copies, waits for them, and re-layouts: 44.4 us -> none  [body(): return mixed.astype(jnp.bfloat16)]
    dot_general x3 -> x0, other arithmetic: 32.9 us -> none  [the longest x1 16.5 us: transform_real(): jnp.dot(sine_neg, source, precision=highest, preferred_element_type=jnp.f...]
    pallas_call x0 -> x1, Pallas kernels: none -> 27.7 us  [mix(): pl.pallas_call(mix_kernel, grid=(kx_rows // TILE,), in_specs=[pl.BlockSpe...]
    reshape x3 -> x1, local copies, waits for them, and re-layouts: 24.3 us -> 0.02 us  [body(): spread = spread_mixing(mixing.reshape(2 * z_rows, 2 * NSHELL))]
  transfers between devices with their start and end apart: 3 -> 16, of which waited for: 3 -> 7; matrix products, arithmetic and copies ran while one was open for 4% -> 48% of each run, Pallas kernels for 0% -> 0%
where the time goes in v1:
time: 325 us; the launch traced here: 321 us
  matrix products  134 us (41%)
  waiting for transfers between devices  85.3 us (26%)
  local copies, waits for them, and re-layouts  31.4 us (10%)
  Pallas kernels  27.7 us (9%)
  other arithmetic  16.5 us (5%)
  between operations  13.6 us (4%)
  starting transfers between devices  12.4 us (4%)
    dot_general x4, matrix products, body(): jnp.dot(rows_x, gridded, precision=high, preferred_element_type=jnp.float32)  57.9 us
    ppermute x8, waiting for transfers between devices, halving_scatter(): lax.ppermute(give, axis, [(i, i ^ step) for i in range(size)])  41.6 us
    reduce_scatter x4, waiting for transfers between devices, body(): summed = lax.psum_scatter(partial, 'ty', scatter_dimension=0, tiled=True)  39.5 us
    dot_general x4, matrix products, body(): jnp.dot(rows_y, gridded, precision=high, preferred_element_type=jnp.float32)  37.8 us
    pallas_call x1, Pallas kernels, mix(): pl.pallas_call(mix_kernel, grid=(kx_rows // TILE,), in_specs=[pl.BlockSpe...  27.7 us
    dot_general x4, matrix products, body(): jnp.einsum('vj,uv->ju', interp_y[s], weighted, preferred_element_type=jnp...  23.5 us
    unnamed x23, local copies, waits for them, and re-layouts  15.2 us
    add x8, other arithmetic, halving_scatter(): keep + lax.ppermute(give, axis, [(i, i ^ step) for i in range(size)])  13 us
  transfers between devices with their start and end apart: 16, of which 7 were waited for; matrix products, arithmetic and copies ran while one was open for 48% of the time, Pallas kernels for 0%

profile of v1, /device:TPU:0, one launch (start us, length us, event | category | flops | bytes accessed | tf_op | source)
XLA Modules:
  0.0 320.8 jit_solution(2803486156699560626)
XLA Ops:
  6.5 2.0 fusion.71
  8.5 5.8 %fusion.10 = f32[512,1024]{1,0:T(8,128)S(1)} fusion(bf16[4,512,1024]{2,1,0:T(8,128)(2,1)} %param.10, f32[4,512,512]{2,1,0:T(8,128)} %param.7, f32[]{:T(128)} %bitcast.8, f32[]{:T(128)} %bitcast.7, f32[]{:T(128)} %bitcast.6, f32[]{:T(128)} %bitcast.5), kind=kOutput, calls=%fused_computation.24 | convolution fusion | flops 538968064 | bytes 7342080 | tf_op jit(solution)/shard_map/vj,uv->ju/dot_general | solution.py:136
  14.3 9.4 %fusion.72 = f32[2048,512]{1,0:T(8,128)S(1)} fusion(f32[2048,1024]{1,0:T(8,128)} %constant.145.clone, f32[512,1024]{1,0:T(8,128)S(1)} %fusion.10), kind=kOutput, calls=%fused_computation.115 | convolution fusion | flops 6442450944 | bytes 14680064 | tf_op jit(solution)/shard_map/dot_general | solution.py:139
  23.7 2.0 copy-done.2
  25.8 0.5 collective-permute-start
  26.4 3.9 %collective-permute-done = f32[2,512,512]{2,1,0:T(8,128)} collective-permute-done((f32[2,512,512]{2,1,0:T(8,128)S(1)}, f32[2,512,512]{2,1,0:T(8,128)}, u32[]{:S(2)}, u32[]{:S(2)}) %collective-permute-start) | collective-permute-done | bytes 2097184 | tf_op jit(solution)/shard_map/ppermute | solution.py:102
  30.3 2.7 bitcast_add_fusion.3
  33.1 3.0 collective-permute-start.1
  36.0 5.8 %fusion.7 = f32[512,1024]{1,0:T(8,128)S(1)} fusion(bf16[4,512,1024]{2,1,0:T(8,128)(2,1)} %param.10, f32[4,512,512]{2,1,0:T(8,128)} %param.7, f32[]{:T(128)} %bitcast.23, f32[]{:T(128)} %bitcast.22, f32[]{:T(128)} %bitcast.21, f32[]{:T(128)} %bitcast.20), kind=kOutput, calls=%fused_computation.21 | convolution fusion | flops 538968064 | bytes 7342080 | tf_op jit(solution)/shard_map/vj,uv->ju/dot_general | solution.py:136
  41.8 9.4 %fusion.74 = f32[2048,512]{1,0:T(8,128)S(1)} fusion(f32[2048,1024]{1,0:T(8,128)} %constant.145.clone, f32[512,1024]{1,0:T(8,128)S(1)} %fusion.7), kind=kOutput, calls=%fused_computation.117 | convolution fusion | flops 6442450944 | bytes 14680064 | tf_op jit(solution)/shard_map/dot_general | solution.py:139
  51.2 2.0 copy-done.3
  53.2 1.5 dynamic-slice_bitcast_fusion.2
  54.7 4.9 %collective-permute-done.1 = f32[1,512,512]{2,1,0:T(8,128)} collective-permute-done((f32[1,512,512]{2,1,0:T(8,128)S(1)}, f32[1,512,512]{2,1,0:T(8,128)}, u32[]{:S(2)}, u32[]{:S(2)}) %collective-permute-start.1) | collective-permute-done | bytes 1048608 | tf_op jit(solution)/shard_map/ppermute | solution.py:102
  59.6 1.4 dynamic-slice_add_fusion.3
  61.0 2.5 convolution_bitcast_fusion.3
  63.5 1.9 copy.10
  65.4 22.1 %fusion.73 = f32[2048,256]{1,0:T(8,128)} fusion(f32[2048,2048]{1,0:T(8,128)} %constant.146.clone, f32[2048,256]{1,0:T(8,128)} %bitcast.128), kind=kOutput, calls=%fused_computation.116 | convolution fusion | flops 6442450944 | bytes 20971520 | tf_op jit(solution)/shard_map/dot_general | solution.py:152
  87.6 2.7 bitcast_add_fusion.2
  90.4 1.8 collective-permute-start.3
  92.2 5.9 %fusion.4 = f32[512,1024]{1,0:T(8,128)S(1)} fusion(bf16[4,512,1024]{2,1,0:T(8,128)(2,1)} %param.10, f32[4,512,512]{2,1,0:T(8,128)} %param.7, f32[]{:T(128)} %bitcast.38, f32[]{:T(128)} %bitcast.37, f32[]{:T(128)} %bitcast.36, f32[]{:T(128)} %bitcast.35), kind=kOutput, calls=%fused_computation.18 | convolution fusion | flops 538968064 | bytes 7342080 | tf_op jit(solution)/shard_map/vj,uv->ju/dot_general | solution.py:136
  98.2 9.4 %fusion.76 = f32[2048,512]{1,0:T(8,128)S(1)} fusion(f32[2048,1024]{1,0:T(8,128)} %constant.145.clone, f32[512,1024]{1,0:T(8,128)S(1)} %fusion.4), kind=kOutput, calls=%fused_computation.119 | convolution fusion | flops 6442450944 | bytes 14680064 | tf_op jit(solution)/shard_map/dot_general | solution.py:139
  107.6 1.6 dynamic-slice_bitcast_fusion.1
  109.2 6.0 %collective-permute-done.3 = f32[1,512,512]{2,1,0:T(8,128)S(1)} collective-permute-done((f32[1,512,512]{2,1,0:T(8,128)S(1)}, f32[1,512,512]{2,1,0:T(8,128)S(1)}, u32[]{:S(2)}, u32[]{:S(2)}) %collective-permute-start.3) | collective-permute-done | bytes 1048608 | tf_op jit(solution)/shard_map/ppermute | solution.py:102
  115.2 0.2 dynamic-slice_add_fusion.2
  115.4 2.5 convolution_bitcast_fusion.2
  117.9 1.9 copy.11
  119.8 11.9 %fusion.75 = f32[2048,256]{1,0:T(8,128)} fusion(f32[2048,2048]{1,0:T(8,128)} %constant.146.clone, f32[2048,256]{1,0:T(8,128)} %bitcast.129), kind=kOutput, calls=%fused_computation.118 | convolution fusion | flops 6442450944 | bytes 20971520 | tf_op jit(solution)/shard_map/dot_general | solution.py:152
  131.7 2.8 bitcast_add_fusion.1
  134.6 1.5 collective-permute-start.5
  136.1 6.0 %fusion.1 = f32[512,1024]{1,0:T(8,128)S(1)} fusion(bf16[4,512,1024]{2,1,0:T(8,128)(2,1)} %param.10, f32[4,512,512]{2,1,0:T(8,128)} %param.7, f32[]{:T(128)} %bitcast.53, f32[]{:T(128)} %bitcast.52, f32[]{:T(128)} %bitcast.51, f32[]{:T(128)} %bitcast.50), kind=kOutput, calls=%fused_computation.15 | convolution fusion | flops 538968064 | bytes 7342080 | tf_op jit(solution)/shard_map/vj,uv->ju/dot_general | solution.py:136
  142.0 9.8 %fusion.78 = f32[2048,512]{1,0:T(8,128)S(1)} fusion(f32[2048,1024]{1,0:T(8,128)} %constant.145.clone, f32[512,1024]{1,0:T(8,128)S(1)} %fusion.1), kind=kOutput, calls=%fused_computation.121 | convolution fusion | flops 6442450944 | bytes 14680064 | tf_op jit(solution)/shard_map/dot_general | solution.py:139
  151.8 1.7 dynamic-slice_bitcast_fusion
  153.5 5.0 %collective-permute-done.5 = f32[1,512,512]{2,1,0:T(8,128)S(1)} collective-permute-done((f32[1,512,512]{2,1,0:T(8,128)S(1)}, f32[1,512,512]{2,1,0:T(8,128)S(1)}, u32[]{:S(2)}, u32[]{:S(2)}) %collective-permute-start.5) | collective-permute-done | bytes 1048608 | tf_op jit(solution)/shard_map/ppermute | solution.py:102
  158.5 0.2 dynamic-slice_add_fusion.1
  158.7 2.5 convolution_bitcast_fusion.1
  161.2 1.8 copy.12
  163.0 11.9 %fusion.77 = f32[2048,256]{1,0:T(8,128)} fusion(f32[2048,2048]{1,0:T(8,128)} %constant.146.clone, f32[2048,256]{1,0:T(8,128)} %bitcast.130), kind=kOutput, calls=%fused_computation.120 | convolution fusion | flops 6442450944 | bytes 20971520 | tf_op jit(solution)/shard_map/dot_general | solution.py:152
  175.0 2.7 bitcast_add_fusion
  177.9 1.2 collective-permute-start.7
  179.1 21.8 %collective-permute-done.7 = f32[1,512,512]{2,1,0:T(8,128)S(1)} collective-permute-done((f32[1,512,512]{2,1,0:T(8,128)S(1)}, f32[1,512,512]{2,1,0:T(8,128)S(1)}, u32[]{:S(2)}, u32[]{:S(2)}) %collective-permute-start.7) | collective-permute-done | bytes 1048608 | tf_op jit(solution)/shard_map/ppermute | solution.py:102
  200.9 0.2 dynamic-slice_add_fusion
  201.1 2.5 convolution_bitcast_fusion
  203.6 2.0 copy.13
  205.6 12.0 %fusion.79 = f32[2048,256]{1,0:T(8,128)} fusion(f32[2048,2048]{1,0:T(8,128)} %constant.146.clone, f32[2048,256]{1,0:T(8,128)} %bitcast.127), kind=kOutput, calls=%fused_computation.122 | convolution fusion | flops 6442450944 | bytes 20971520 | tf_op jit(solution)/shard_map/dot_general | solution.py:152
  217.8 2.3 convolution_bitcast_fusion.4
  220.1 2.4 fusion.39
  222.9 0.2 copy.9
  223.1 0.8 collective-permute-start.8
  224.0 3.4 %multiply_convert_fusion = bf16[512,16,256]{2,1,0:T(8,128)(2,1)} fusion(f32[16,256]{1,0:T(8,128)S(1)} %tile.9, f32[512,256]{1,0:T(8,128)S(1)} %copy.9), kind=kLoop, calls=%fused_computation | loop fusion | flops 4194304 | bytes 4734976 | tf_op jit(solution)/shard_map/convert_element_type | solution.py:73
  227.3 1.2 collective-permute-start.9
  228.6 0.8 constant_dynamic-update-slice_fusion.7
  229.4 0.8 collective-permute-start.10
  230.2 39.5 %reduce-scatter.11.cloned.1.call-done = f32[512,256]{1,0:T(8,128)} async-done(((f32[2048,256]{1,0:T(8,128)}), f32[512,256]{1,0:T(8,128)}) %reduce-scatter.11.cloned.1.call-update) | async-done | bytes 524304 | tf_op jit(solution)/shard_map/reduce_scatter | solution.py:153
  269.7 1.5 collective-permute-start.11
  271.1 1.9 constant_dynamic-update-slice_fusion.6
  273.0 1.9 constant_dynamic-update-slice_fusion.5
  274.9 1.9 constant_dynamic-update-slice_fusion.4
  276.8 0.8 constant_dynamic-update-slice_fusion.3
  277.6 0.8 constant_dynamic-update-slice_fusion.2
  278.4 0.8 constant_dynamic-update-slice_fusion.1
  279.3 4.1 %collective-permute-done.11 = f32[2,256,256]{2,1,0:T(8,128)S(1)} collective-permute-done((f32[2,256,256]{2,1,0:T(8,128)}, f32[2,256,256]{2,1,0:T(8,128)S(1)}, u32[]{:S(2)}, u32[]{:S(2)}) %collective-permute-start.11) | collective-permute-done | bytes 524320 | tf_op jit(solution)/shard_map/ppermute | solution.py:158
  283.4 0.8 constant_dynamic-update-slice_fusion.spec_ref
  284.2 2.2 copy-done.1
  286.4 27.7 %shard_map.73 = bf16[512,256,256]{2,1,0:T(8,128)(2,1)} custom-call(bf16[8192,256]{1,0:T(8,128)(2,1)S(1)} %bitcast.126, f32[16,256,256]{2,1,0:T(8,128)S(1)} %copy-done.1), custom_call_target="tpu_custom_call" | custom-call | tf_op jit(solution)/shard_map/pallas_call | solution.py:79
  (50 shorter events, 1.2 us)
Async XLA Ops:
  6.5 216.6 %reduce-scatter.5.cloned.1.call-start = ((), (), s32[]{:S(2)}) async-start(), calls=%async_computation.4 | async-start | bytes 2621440 | tf_op jit(solution)/shard_map/reduce_scatter | solution.py:153
  23.6 2.0 copy-start.2
  25.8 4.4 %collective-permute-start = (f32[2,512,512]{2,1,0:T(8,128)S(1)}, f32[2,512,512]{2,1,0:T(8,128)}, u32[]{:S(2)}, u32[]{:S(2)}) collective-permute-start(f32[2,512,512]{2,1,0:T(8,128)S(1)} %dynamic-slice_bitcast_fusion.3), channel_id=1, source_target_pairs={{0,4},{4,0},{8,12},{12,8},{1,5},{5,1},{9,13},{13,9},{2,6},{6,2},{1... | collective-permute-start | bytes 6291464 | tf_op jit(solution)/shard_map/ppermute | solution.py:102
  33.1 26.5 %collective-permute-start.1 = (f32[1,512,512]{2,1,0:T(8,128)S(1)}, f32[1,512,512]{2,1,0:T(8,128)}, u32[]{:S(2)}, u32[]{:S(2)}) collective-permute-start(f32[1,512,512]{2,1,0:T(8,128)S(1)} %constant_dynamic-slice_fusion.3), channel_id=1, source_target_pairs={{0,8},{4,12},{8,0},{12,4},{1,9},{5,13},{9,1},{13,5},{2,10},{6,14},... | collective-permute-start | bytes 3145736 | tf_op jit(solution)/shard_map/ppermute | solution.py:102
  51.2 2.0 copy-start.3
  54.7 32.9 %collective-permute-start.2 = (f32[2,512,512]{2,1,0:T(8,128)}, f32[2,512,512]{2,1,0:T(8,128)}, u32[]{:S(2)}, u32[]{:S(2)}) collective-permute-start(f32[2,512,512]{2,1,0:T(8,128)} %dynamic-slice_bitcast_fusion.2), channel_id=1, source_target_pairs={{0,4},{4,0},{8,12},{12,8},{1,5},{5,1},{9,13},{13,9},{2,6},{6,2},{1... | collective-permute-start | bytes 6291464 | tf_op jit(solution)/shard_map/ppermute | solution.py:102
  87.6 139.8 %reduce-scatter.7.cloned.1.call-start = ((), (), s32[]{:S(2)}) async-start(), calls=%async_computation.5 | async-start | bytes 2621440 | tf_op jit(solution)/shard_map/reduce_scatter | solution.py:153
  90.4 24.8 %collective-permute-start.3 = (f32[1,512,512]{2,1,0:T(8,128)S(1)}, f32[1,512,512]{2,1,0:T(8,128)S(1)}, u32[]{:S(2)}, u32[]{:S(2)}) collective-permute-start(f32[1,512,512]{2,1,0:T(8,128)S(1)} %constant_dynamic-slice_fusion.2), channel_id=1, source_target_pairs={{0,8},{4,12},{8,0},{12,4},{1,9},{5,13},{9,1},{13,5},{2,10},{6,14},... | collective-permute-start | bytes 3145736 | tf_op jit(solution)/shard_map/ppermute | solution.py:102
  107.5 7.8 %copy-start.5 = (f32[2048,512]{1,0:T(8,128)}, f32[2048,512]{1,0:T(8,128)S(1)}, u32[]{:S(2)}) copy-start(f32[2048,512]{1,0:T(8,128)S(1)} %fusion.76) | copy-start | bytes 12582916
  109.2 22.5 %collective-permute-start.4 = (f32[2,512,512]{2,1,0:T(8,128)}, f32[2,512,512]{2,1,0:T(8,128)}, u32[]{:S(2)}, u32[]{:S(2)}) collective-permute-start(f32[2,512,512]{2,1,0:T(8,128)} %dynamic-slice_bitcast_fusion.1), channel_id=1, source_target_pairs={{0,4},{4,0},{8,12},{12,8},{1,5},{5,1},{9,13},{13,9},{2,6},{6,2},{1... | collective-permute-start | bytes 6291464 | tf_op jit(solution)/shard_map/ppermute | solution.py:102
  131.7 97.7 %reduce-scatter.9.cloned.1.call-start = ((), (), s32[]{:S(2)}) async-start(), calls=%async_computation.6 | async-start | bytes 2621440 | tf_op jit(solution)/shard_map/reduce_scatter | solution.py:153
  134.6 23.9 %collective-permute-start.5 = (f32[1,512,512]{2,1,0:T(8,128)S(1)}, f32[1,512,512]{2,1,0:T(8,128)S(1)}, u32[]{:S(2)}, u32[]{:S(2)}) collective-permute-start(f32[1,512,512]{2,1,0:T(8,128)S(1)} %constant_dynamic-slice_fusion.1), channel_id=1, source_target_pairs={{0,8},{4,12},{8,0},{12,4},{1,9},{5,13},{9,1},{13,5},{2,10},{6,14},... | collective-permute-start | bytes 3145736 | tf_op jit(solution)/shard_map/ppermute | solution.py:102
  151.8 6.9 %copy-start.4 = (f32[2048,512]{1,0:T(8,128)}, f32[2048,512]{1,0:T(8,128)S(1)}, u32[]{:S(2)}) copy-start(f32[2048,512]{1,0:T(8,128)S(1)} %fusion.78) | copy-start | bytes 12582916
  153.5 21.5 %collective-permute-start.6 = (f32[2,512,512]{2,1,0:T(8,128)}, f32[2,512,512]{2,1,0:T(8,128)}, u32[]{:S(2)}, u32[]{:S(2)}) collective-permute-start(f32[2,512,512]{2,1,0:T(8,128)} %dynamic-slice_bitcast_fusion), channel_id=1, source_target_pairs={{0,4},{4,0},{8,12},{12,8},{1,5},{5,1},{9,13},{13,9},{2,6},{6,2},{1... | collective-permute-start | bytes 6291464 | tf_op jit(solution)/shard_map/ppermute | solution.py:102
  175.0 94.7 %reduce-scatter.11.cloned.1.call-start = ((), (), s32[]{:S(2)}) async-start(), calls=%async_computation.7 | async-start | bytes 2621440 | tf_op jit(solution)/shard_map/reduce_scatter | solution.py:153
  177.9 23.0 %collective-permute-start.7 = (f32[1,512,512]{2,1,0:T(8,128)S(1)}, f32[1,512,512]{2,1,0:T(8,128)S(1)}, u32[]{:S(2)}, u32[]{:S(2)}) collective-permute-start(f32[1,512,512]{2,1,0:T(8,128)S(1)} %constant_dynamic-slice_fusion), channel_id=1, source_target_pairs={{0,8},{4,12},{8,0},{12,4},{1,9},{5,13},{9,1},{13,5},{2,10},{6,14},... | collective-permute-start | bytes 3145736 | tf_op jit(solution)/shard_map/ppermute | solution.py:102
  205.6 12.2 %copy-start.7 = (s32[512]{0:T(512)S(1)}, s32[512]{0:T(512)}, u32[]{:S(2)}) copy-start(s32[512]{0:T(512)} %param.11) | copy-start | bytes 6148
  223.1 5.5 %copy-start.6 = (f32[512,256]{1,0:T(8,128)S(1)}, f32[512,256]{1,0:T(8,128)}, u32[]{:S(2)}) copy-start(f32[512,256]{1,0:T(8,128)} %reduce-scatter.5.cloned.1.call-done) | copy-start | bytes 1572868
  223.1 53.7 %collective-permute-start.8 = (f32[2,256,256]{2,1,0:T(8,128)}, f32[2,256,256]{2,1,0:T(8,128)S(1)}, u32[]{:S(2)}, u32[]{:S(2)}) collective-permute-start(f32[2,256,256]{2,1,0:T(8,128)} %bitcast.144), channel_id=1, source_target_pairs={{16,0},{0,16},{17,1},{1,17},{18,2},{2,18},{19,3},{3,19},{20,4},{4,... | collective-permute-start | bytes 1572872 | tf_op jit(solution)/shard_map/ppermute | solution.py:158
  227.3 50.3 %collective-permute-start.9 = (f32[2,256,256]{2,1,0:T(8,128)}, f32[2,256,256]{2,1,0:T(8,128)S(1)}, u32[]{:S(2)}, u32[]{:S(2)}) collective-permute-start(f32[2,256,256]{2,1,0:T(8,128)} %bitcast.146), channel_id=1, source_target_pairs={{16,0},{0,16},{17,1},{1,17},{18,2},{2,18},{19,3},{3,19},{20,4},{4,... | collective-permute-start | bytes 1572872 | tf_op jit(solution)/shard_map/ppermute | solution.py:158
  229.4 49.0 %collective-permute-start.10 = (f32[2,256,256]{2,1,0:T(8,128)}, f32[2,256,256]{2,1,0:T(8,128)S(1)}, u32[]{:S(2)}, u32[]{:S(2)}) collective-permute-start(f32[2,256,256]{2,1,0:T(8,128)} %bitcast.148), channel_id=1, source_target_pairs={{16,0},{0,16},{17,1},{1,17},{18,2},{2,18},{19,3},{3,19},{20,4},{4,... | collective-permute-start | bytes 1572872 | tf_op jit(solution)/shard_map/ppermute | solution.py:158
  269.7 14.5 %copy-start = (bf16[512,16,256]{2,1,0:T(8,128)(2,1)S(1)}, bf16[512,16,256]{2,1,0:T(8,128)(2,1)}, u32[]{:S(2)}) copy-start(bf16[512,16,256]{2,1,0:T(8,128)(2,1)} %multiply_convert_fusion) | copy-start | bytes 12582916
  269.7 13.7 %collective-permute-start.11 = (f32[2,256,256]{2,1,0:T(8,128)}, f32[2,256,256]{2,1,0:T(8,128)S(1)}, u32[]{:S(2)}, u32[]{:S(2)}) collective-permute-start(f32[2,256,256]{2,1,0:T(8,128)} %bitcast.150), channel_id=1, source_target_pairs={{16,0},{0,16},{17,1},{1,17},{18,2},{2,18},{19,3},{3,19},{20,4},{4,... | collective-permute-start | bytes 1572872 | tf_op jit(solution)/shard_map/ppermute | solution.py:158
  284.2 2.2 copy-start.1
Sparse Core Ops, SparseCore 0:
  87.7 45.3 reduce-scatter.4
  135.5 43.1 reduce-scatter.6
  181.0 43.1 reduce-scatter.8
  226.5 43.1 reduce-scatter.10
